TPU v7x, 128 devices: a whole 4x4x4 slice. The times are simulated.
128 devices in a mesh: dp: 8 (over z, y_hi), ctx: 16 (over x, y_lo, core).
Axes of the slice: x: 4, y: 4 (y_hi: 2, y_lo: 2; y = y_hi * 2 + y_lo), z: 4, core: 2. Of those that a mesh axis runs over, the one named last changes fastest.
Arguments:
- inputs: bfloat16 [8, 4096, 1536], P('dp', 'ctx'), may hold values from -6 to 6
- block_ids: int32 [8, 32], P('dp'), may hold values from 0 to 2, never falling along the last dimension, each value on 1 to 24 neighbouring positions
- attn_gain: float32 [1536], replicated, may hold values from 0.1 to 1.9
- w_qkv: bfloat16 [1536, 2304], replicated, may hold values from -6 to 6
- w_out: bfloat16 [768, 1536], replicated, may hold values from -0.21875 to 0.21875
- conv_gain: float32 [1536], replicated, may hold values from 0.1 to 1.9
- conv_in: bfloat16 [1536, 3072], P(None, 'dp'), may hold values from -0.15625 to 0.15625
- depthwise_w: float32 [31, 1536], replicated, may hold values from -1 to 1
- depth_gain: float32 [1536], replicated, may hold values from 0.1 to 1.9
- conv_out: bfloat16 [1536, 1536], replicated, may hold values from -0.15625 to 0.15625
Outputs:
- output: bfloat16 [8, 4096, 1536], P('dp', 'ctx')
Inputs may be any that keep to these rules, and one draw needn't show every extreme that they name: `block_ids`: utterance numbers never fall along a row; a row holds 3 utterances of 1 to 24 blocks, one of exactly 24 blocks.
All inputs are finite; a program needn't handle non-finite values.
Results may differ from a plain program's by a relative error of at most 0.01.
Values may be sent and summed in bfloat16 or wider, within the bound.
A program may use at most 192 MiB of HBM per device.

v0:
```python
import math

import jax
import jax.numpy as jnp
from jax import lax
from jax.sharding import PartitionSpec as P

MODEL_DIM = 1536
HEAD_COUNT = 8
HEAD_DIM = 96
KERNEL = 31
BLOCK_LEN = 128


EPSILON = 1e-05


def extended_2(shard, sides, width):
    for axis, dim in sides:
        size, length = (lax.axis_size(axis), shard.shape[dim])
        up = [(i, (i + 1) % size) for i in range(size - 1)]
        down = [(j, i) for i, j in up]
        last = lax.slice_in_dim(shard, length - width, length, axis=dim)
        initial = lax.slice_in_dim(shard, 0, width, axis=dim)
        before = lax.ppermute(last, axis, up)
        after = lax.ppermute(initial, axis, down)
        shard = jnp.concatenate([before, shard, after], axis=dim)
    return shard


def layer_norm(values, weights):
    values = values.astype(jnp.float32)
    average = jnp.mean(values, axis=-1, keepdims=True)
    centred = values - average
    variance = jnp.mean(centred * centred, axis=-1, keepdims=True)
    return centred * lax.rsqrt(variance + EPSILON) * weights


def frame_tables(row_ids):
    earlier = jnp.sum((row_ids[None, :] < row_ids[:, None]).astype(jnp.int32), axis=1)
    frame_utt = jnp.repeat(row_ids, BLOCK_LEN)
    first_frame = jnp.repeat(earlier, BLOCK_LEN) * BLOCK_LEN
    positions = jnp.arange(frame_utt.shape[0], dtype=jnp.int32) - first_frame
    return (frame_utt, positions)


def rotate(values, positions):
    half_dim = values.shape[-1] // 2
    inverse = 10000.0 ** (-jnp.arange(half_dim, dtype=jnp.float32) / half_dim)
    angles = positions.astype(jnp.float32)[:, None] * inverse[None, :]
    cosine = jnp.cos(angles)[:, None, :]
    sine_table = jnp.sin(angles)[:, None, :]
    first_half = values[..., :half_dim]
    second = values[..., half_dim:]
    return jnp.concatenate(
        [first_half * cosine - second * sine_table, second * cosine + first_half * sine_table],
        axis=-1,
    )


def project(normed, w_qkv, positions):
    projected = jnp.dot(normed, w_qkv, preferred_element_type=jnp.float32)
    shaped = projected.reshape(projected.shape[0], 3, HEAD_COUNT, HEAD_DIM)
    queries = rotate(shaped[:, 0], positions).astype(jnp.bfloat16)
    key_rows = rotate(shaped[:, 1], positions).astype(jnp.bfloat16)
    value_rows = shaped[:, 2].astype(jnp.bfloat16)
    return (queries, key_rows, value_rows)


def depthwise(extended, local_utt, extended_utt, kernel_weights):
    length = local_utt.shape[0]
    result = jnp.zeros((length, extended.shape[1]), jnp.float32)
    for shift_tap in range(KERNEL):
        same_utt = (extended_utt[shift_tap : shift_tap + length] == local_utt)[:, None]
        term = kernel_weights[shift_tap][None, :] * extended[shift_tap : shift_tap + length].astype(
            jnp.float32
        )
        result = result + jnp.where(same_utt, term, 0.0)
    return result


def local(
    inputs,
    block_ids,
    attn_gain,
    w_qkv,
    w_out,
    conv_gain,
    conv_in,
    depthwise_w,
    depth_gain,
    conv_out,
):
    frames_here = inputs.shape[1]
    device = lax.axis_index("ctx")
    my_offset = device * frames_here
    frame_utt, positions = frame_tables(block_ids[0])
    local_utt = lax.dynamic_slice_in_dim(frame_utt, my_offset, frames_here)
    local_positions = lax.dynamic_slice_in_dim(positions, my_offset, frames_here)
    row_inputs = inputs[0]
    normed = layer_norm(row_inputs, attn_gain).astype(jnp.bfloat16)
    queries, key_rows, value_rows = project(normed, w_qkv, local_positions)
    stacked = jnp.stack([key_rows.reshape(frames_here, -1), value_rows.reshape(frames_here, -1)])
    score_scale = 1.0 / math.sqrt(HEAD_DIM)
    pieces = lax.all_gather(stacked, "ctx", axis=1, tiled=True)
    length = pieces.shape[1]
    allowed = local_utt[:, None] == frame_utt[None, :]
    row_max = jnp.full((HEAD_COUNT, frames_here), -1e30, jnp.float32)
    key_piece = pieces[0].reshape(length, HEAD_COUNT, HEAD_DIM)
    value_piece = pieces[1].reshape(length, HEAD_COUNT, HEAD_DIM)
    scores = (
        jnp.einsum("qhd,khd->hqk", queries, key_piece, preferred_element_type=jnp.float32)
        * score_scale
    )
    scores = jnp.where(allowed[None], scores, -jnp.inf)
    new_max = jnp.maximum(row_max, jnp.max(scores, axis=-1))
    exp_scores = jnp.exp(scores - new_max[:, :, None])
    row_sum = jnp.sum(exp_scores, axis=-1)
    product = jnp.einsum(
        "hqk,khd->qhd",
        exp_scores.astype(jnp.bfloat16),
        value_piece,
        preferred_element_type=jnp.float32,
    )
    weighted = product
    running = (new_max, row_sum, weighted)
    row_max, row_sum, weighted = running
    attended = (
        (weighted / jnp.transpose(row_sum)[:, :, None])
        .reshape(frames_here, -1)
        .astype(jnp.bfloat16)
    )
    residual = row_inputs.astype(jnp.float32) + jnp.dot(
        attended, w_out, preferred_element_type=jnp.float32
    )
    conv_normed = layer_norm(residual, conv_gain).astype(jnp.bfloat16)
    widened = jnp.dot(
        conv_normed,
        lax.all_gather(conv_in, "dp", axis=1, tiled=True),
        preferred_element_type=jnp.float32,
    )
    gated = (widened[:, :MODEL_DIM] * jax.nn.sigmoid(widened[:, MODEL_DIM:])).astype(jnp.bfloat16)
    half_kernel = KERNEL // 2
    extended = extended_2(gated[None], (("ctx", 1),), half_kernel)[0]
    padded_utt = jnp.pad(frame_utt, (half_kernel, half_kernel), constant_values=-1)
    extended_utt = lax.dynamic_slice_in_dim(padded_utt, my_offset, frames_here + 2 * half_kernel)
    filtered = depthwise(extended, local_utt, extended_utt, depthwise_w)
    activated = jax.nn.silu(layer_norm(filtered, depth_gain)).astype(jnp.bfloat16)
    output = residual + jnp.dot(activated, conv_out, preferred_element_type=jnp.float32)
    return output.astype(jnp.bfloat16)[None]


def solution(mesh):
    return jax.shard_map(
        local,
        mesh=mesh,
        in_specs=(
            P("dp", "ctx", None),
            P("dp", None),
            P(),
            P(),
            P(),
            P(),
            P(None, "dp"),
            P(),
            P(),
            P(),
        ),
        out_specs=P("dp", "ctx", None),
        check_vma=False,
    )
```

profile of v0, /device:TPU:0, one launch (start us, length us, event | category | flops | bytes accessed | tf_op | source)
XLA Modules:
  0.0 279.6 jit_solution(11116332907920689676)
XLA Ops:
  6.5 0.0 all-gather.3.cloned.1.call-start
  6.5 10.4 %copy.13 = bf16[1536,2304]{0,1:T(8,128)(2,1)} copy(bf16[1536,2304]{1,0:T(8,128)(2,1)} %param.13) | data formatting | bytes 14155776 | tf_op args[3]
  17.0 0.2 convert_reduce_fusion
  17.2 0.3 fusion.10
  17.5 0.1 copy-done.40
  17.7 5.3 %fusion.90 = f32[256,3,8,96]{0,3,2,1:T(8,128)S(1)} fusion(bf16[3,8,96,1536]{3,2,1,0:T(8,128)(2,1)} %bitcast.233, bf16[1,256,1536]{2,1,0:T(8,128)(2,1)S(1)} %copy-done.1, f32[1536]{0:T(1024)S(1)} %copy-done.40, f32[256]{0:T(256)S(1)} %add_rsqrt_fusion.2, f32[256]{0:T(256)S(1)} %broadcast_multiply_fusion.2), kind=kOutput, calls=%fused_computation.154 | convolution fusion | flops 1813905408 | bytes 10231808 | tf_op jit(solution)/shard_map/dot_general | solution.py:62
  23.0 0.0 copy-start.38
  23.0 1.0 slice_bitcast_fusion
  24.0 0.6 multiply_power_fusion
  24.6 0.2 convert_reduce_fusion.1
  24.8 0.1 broadcast_bitcast_fusion.1
  24.8 0.1 fusion.164
  24.9 0.9 multiply_cosine_fusion
  25.9 2.1 subtract_convert_fusion
  28.0 0.0 copy-start.39
  28.0 0.0 copy-start.4
  28.0 0.9 pad_maximum_fusion.2
  29.0 0.0 all-gather.3.cloned.1.call-update
  29.0 0.0 all-gather.5.cloned.1.call-start
  29.0 0.7 all-gather.5.cloned.1.call-update
  29.8 0.1 broadcast_bitcast_fusion
  29.8 0.1 pad_dynamic-slice_fusion
  29.9 0.9 slice_reduce_fusion.30
  30.8 0.6 slice_compare_fusion.30
  31.4 0.7 slice_compare_fusion.28
  32.1 0.7 slice_compare_fusion.29
  32.9 0.6 broadcast_compare_fusion
  33.5 77.5 %all-gather.3.cloned.1.call-done = bf16[2,4096,768]{1,2,0:T(8,128)(2,1)} async-done(((bf16[2,256,768]{1,2,0:T(8,128)(2,1)}), bf16[2,4096,768]{1,2,0:T(8,128)(2,1)}) %all-gather.3.cloned.1.call-update) | async-done | bytes 12582928 | tf_op jit(solution)/shard_map/all_gather | solution.py:105
  111.1 8.4 %fusion.171 = (bf16[1,4096,768]{1,2,0:T(8,128)(2,1)S(1)}, bf16[1,4096,768]{1,2,0:T(8,128)(2,1)}) fusion(bf16[2,4096,768]{1,2,0:T(8,128)(2,1)} %all-gather.3.cloned.1.call-done), kind=kLoop, calls=%fused_computation.339 | loop fusion | bytes 25165824 | tf_op jit(solution)/shard_map/slice | solution.py:109
  119.5 15.5 %fusion = (f32[8,256]{1,0:T(8,128)S(1)}, f32[8,256,4096]{2,1,0:T(8,128)}) fusion(pred[256,4096]{1,0:T(8,128)(4,1)S(1)} %broadcast_compare_fusion, bf16[4096,8,96]{0,2,1:T(8,128)(2,1)S(1)} %bitcast.232, bf16[256,8,48]{0,2,1:T(8,128)(2,1)} %get-tuple-element.45, bf16[256,8,48]{0,2,1:T(8,128)(2,1)} %get-tuple-element.44), kind=kOutput, calls=%fused_computation.2 | convolution fusion | flops 1636562944 | bytes 41295872 | tf_op jit(solution)/shard_map/qhd,khd->hqk/dot_general | solution.py:112
  134.9 16.1 %fusion.1 = f32[8,256]{1,0:T(8,128)} fusion(f32[8,256,4096]{2,1,0:T(8,128)} %get-tuple-element.85, f32[8,256]{1,0:T(8,128)S(1)} %broadcast_maximum_fusion, pred[256,4096]{1,0:T(8,128)(4,1)S(1)} %broadcast_compare_fusion), kind=kLoop, calls=%fused_computation.3 | loop fusion | flops 33552384 | bytes 34619392 | tf_op jit(solution)/shard_map/reduce_sum | solution.py:118
  151.1 0.0 copy-done.6
  151.1 17.4 %fusion.85 = bf16[256,8,96]{0,2,1:T(8,128)(2,1)} fusion(bf16[4096,8,96]{0,2,1:T(8,128)(2,1)} %bitcast.234, f32[8,256,4096]{2,1,0:T(8,128)} %get-tuple-element.85, f32[8,256]{1,0:T(8,128)} %copy-done.6, pred[256,4096]{1,0:T(8,128)(4,1)S(1)} %broadcast_compare_fusion, f32[256,8]{0,1:T(8,128)} %bitcast.238), kind=kOutput, calls=%fused_computation.151 | convolution fusion | flops 1644560384 | bytes 41304064 | tf_op jit(solution)/shard_map/hqk,khd->qhd/dot_general | solution.py:119
  168.4 2.2 fusion.173
  170.6 0.0 copy-start.41
  170.6 1.1 copy-done.2
  171.8 0.3 multiply_reduce_fusion.1
  172.1 64.9 %all-gather.5.cloned.1.call-done = bf16[1536,3072]{1,0:T(8,128)(2,1)} async-done(((bf16[1536,384]{1,0:T(8,128)(2,1)}), bf16[1536,3072]{1,0:T(8,128)(2,1)}) %all-gather.5.cloned.1.call-update) | async-done | bytes 9437200 | tf_op jit(solution)/shard_map/all_gather | solution.py:139
  237.0 0.0 copy-done.41
  237.0 5.7 %fusion.88 = f32[256,3072]{1,0:T(8,128)S(1)} fusion(bf16[1536,3072]{1,0:T(8,128)(2,1)} %all-gather.5.cloned.1.call-done, f32[256,1536]{1,0:T(8,128)} %copy-done.2, f32[1536]{0:T(1024)S(1)} %copy-done.41, f32[256]{0:T(256)S(1)} %add_rsqrt_fusion.1, f32[256]{0:T(256)S(1)} %broadcast_multiply_fusion.1), kind=kOutput, calls=%fused_computation.152 | convolution fusion | flops 2417491968 | bytes 14163968 | tf_op jit(solution)/shard_map/dot_general | solution.py:137
  243.1 0.4 fusion.181
  243.5 1.3 collective-permute-start.1
  244.8 3.0 %collective-permute-start = (bf16[1,15,1536]{2,1,0:T(8,128)(2,1)S(1)}, bf16[1,15,1536]{2,1,0:T(8,128)(2,1)S(1)}, u32[]{:S(2)}, u32[]{:S(2)}) collective-permute-start(bf16[1,15,1536]{2,1,0:T(8,128)(2,1)S(1)} %get-tuple-element.48), channel_id=1, source_target_pairs={{0,1},{1,2},{2,3},{3,4},{4,5},{5,6},{6,7},{7,8},{8,9},{9,10},{10,1... | collective-permute-start | bytes 138248 | tf_op jit(solution)/shard_map/ppermute | solution.py:25
  247.9 1.5 slice_reduce_fusion.29
  249.4 0.0 collective-permute-done.1
  249.4 0.0 collective-permute-done
  249.4 0.0 copy-done.5
  249.4 0.0 copy-done.7
  249.4 0.0 copy-done.8
  249.4 0.0 copy-done.9
  249.4 0.0 copy-done.10
  249.4 0.0 copy-done.11
  249.4 0.0 copy-done.12
  249.4 0.0 copy-done.13
  249.5 0.0 copy-done.14
  249.5 0.0 copy-done.15
  249.5 0.0 copy-done.16
  249.5 0.0 copy-done.17
  249.5 0.0 copy-done.18
  249.7 16.9 %fusion.169 = (f32[256]{0:T(256)S(1)}, f32[256,1536]{1,0:T(8,128)S(1)}) fusion(bf16[1,15,1536]{2,1,0:T(8,128)(2,1)S(1)} %collective-permute-done.1, bf16[1,256,1536]{2,1,0:T(8,128)(2,1)S(1)} %fusion.181, f32[1536]{0:T(1024)S(1)} %get-tuple-element.34, pred[256]{0:T(512)(128)(4,1)S(1)} %copy-done.36, f32[1536]{0:T(1024)S(1)} %get-tuple-element.35, ...), kind=kLoop, calls=%fused_computation.338 | loop fusion | flops 97910528 | bytes 5796608 | tf_op jit(solution)/shard_map/reduce_sum | solution.py:33
  266.6 0.0 copy-start.42
  266.7 0.3 multiply_reduce_fusion
  267.0 1.1 copy-done.3
  268.0 4.8 %fusion.7 = bf16[1,256,1536]{2,1,0:T(8,128)(2,1)} fusion(f32[256,1536]{1,0:T(8,128)S(1)} %copy-done.3, bf16[1536,1536]{1,0:T(8,128)(2,1)} %param.19, f32[256,1536]{1,0:T(8,128)S(1)} %get-tuple-element.37, f32[1536]{0:T(1024)S(1)} %copy-done.42, f32[256]{0:T(256)S(1)} %add_rsqrt_fusion, f32[256]{0:T(256)S(1)} %broadcast_multiply_fusion), kind=kOutput, calls=%fused_computation.38 | convolution fusion | flops 1211891712 | bytes 8658944 | tf_op jit(solution)/shard_map/dot_general | solution.py:149
  (74 shorter events, 0.3 us)
Async XLA Ops:
  6.5 161.9 %copy-start = (bf16[768,1536]{1,0:T(8,128)(2,1)S(1)}, bf16[768,1536]{1,0:T(8,128)(2,1)}, u32[]{:S(2)}) copy-start(bf16[768,1536]{1,0:T(8,128)(2,1)} %param.14) | copy-start | bytes 7077892
  6.5 10.4 %copy-start.1 = (bf16[1,256,1536]{2,1,0:T(8,128)(2,1)S(1)}, bf16[1,256,1536]{2,1,0:T(8,128)(2,1)}, u32[]{:S(2)}) copy-start(bf16[1,256,1536]{2,1,0:T(8,128)(2,1)} %param.10) | copy-start | bytes 2359300
  6.5 104.5 %all-gather.3.cloned.1.call-start = ((), (), s32[]{:S(2)}) async-start(), calls=%async_computation | async-start | bytes 13369344 | tf_op jit(solution)/shard_map/all_gather | solution.py:105
  17.0 0.7 copy-start.40
  23.0 1.6 copy-start.38
  28.0 1.8 copy-start.39
  28.0 1.9 copy-start.4
  29.0 208.0 %all-gather.5.cloned.1.call-start = ((), (), s32[]{:S(2)}) async-start(), calls=%async_computation.1 | async-start | bytes 10616832 | tf_op jit(solution)/shard_map/all_gather | solution.py:139
  134.9 16.1 %copy-start.6 = (f32[8,256]{1,0:T(8,128)}, f32[8,256]{1,0:T(8,128)S(1)}, u32[]{:S(2)}) copy-start(f32[8,256]{1,0:T(8,128)S(1)} %broadcast_maximum_fusion) | copy-start | bytes 24580
  170.6 1.2 copy-start.2
  170.6 66.4 %copy-start.41 = (f32[1536]{0:T(1024)S(1)}, f32[1536]{0:T(1024)}, u32[]{:S(2)}) copy-start(f32[1536]{0:T(1024)} %param.15) | copy-start | bytes 18436
  242.7 6.6 %copy-start.5 = (f32[1536]{0:T(1024)S(1)}, f32[1536]{0:T(1024)}, u32[]{:S(2)}) copy-start(f32[1536]{0:T(1024)} %get-tuple-element.23) | copy-start | bytes 18436
  242.8 6.6 %copy-start.7 = (pred[256]{0:T(512)(128)(4,1)S(1)}, pred[256]{0:T(512)(128)(4,1)}, u32[]{:S(2)}) copy-start(pred[256]{0:T(512)(128)(4,1)} %get-tuple-element.52) | copy-start | bytes 772
  242.8 6.6 %copy-start.8 = (pred[256]{0:T(512)(128)(4,1)S(1)}, pred[256]{0:T(512)(128)(4,1)}, u32[]{:S(2)}) copy-start(pred[256]{0:T(512)(128)(4,1)} %get-tuple-element.53) | copy-start | bytes 772
  242.8 6.6 %copy-start.9 = (pred[256]{0:T(512)(128)(4,1)S(1)}, pred[256]{0:T(512)(128)(4,1)}, u32[]{:S(2)}) copy-start(pred[256]{0:T(512)(128)(4,1)} %get-tuple-element.54) | copy-start | bytes 772
  242.8 6.6 %copy-start.10 = (pred[256]{0:T(512)(128)(4,1)S(1)}, pred[256]{0:T(512)(128)(4,1)}, u32[]{:S(2)}) copy-start(pred[256]{0:T(512)(128)(4,1)} %get-tuple-element.55) | copy-start | bytes 772
  242.8 6.6 %copy-start.11 = (pred[256]{0:T(512)(128)(4,1)S(1)}, pred[256]{0:T(512)(128)(4,1)}, u32[]{:S(2)}) copy-start(pred[256]{0:T(512)(128)(4,1)} %get-tuple-element.56) | copy-start | bytes 772
  242.8 6.6 %copy-start.12 = (pred[256]{0:T(512)(128)(4,1)S(1)}, pred[256]{0:T(512)(128)(4,1)}, u32[]{:S(2)}) copy-start(pred[256]{0:T(512)(128)(4,1)} %get-tuple-element.57) | copy-start | bytes 772
  242.8 6.6 %copy-start.13 = (pred[256]{0:T(512)(128)(4,1)S(1)}, pred[256]{0:T(512)(128)(4,1)}, u32[]{:S(2)}) copy-start(pred[256]{0:T(512)(128)(4,1)} %get-tuple-element.58) | copy-start | bytes 772
  242.8 6.6 %copy-start.14 = (pred[256]{0:T(512)(128)(4,1)S(1)}, pred[256]{0:T(512)(128)(4,1)}, u32[]{:S(2)}) copy-start(pred[256]{0:T(512)(128)(4,1)} %get-tuple-element.59) | copy-start | bytes 772
  242.8 6.6 %copy-start.15 = (pred[256]{0:T(512)(128)(4,1)S(1)}, pred[256]{0:T(512)(128)(4,1)}, u32[]{:S(2)}) copy-start(pred[256]{0:T(512)(128)(4,1)} %get-tuple-element.60) | copy-start | bytes 772
  242.8 6.6 %copy-start.16 = (pred[256]{0:T(512)(128)(4,1)S(1)}, pred[256]{0:T(512)(128)(4,1)}, u32[]{:S(2)}) copy-start(pred[256]{0:T(512)(128)(4,1)} %get-tuple-element.61) | copy-start | bytes 772
  242.9 6.6 %copy-start.17 = (pred[256]{0:T(512)(128)(4,1)S(1)}, pred[256]{0:T(512)(128)(4,1)}, u32[]{:S(2)}) copy-start(pred[256]{0:T(512)(128)(4,1)} %get-tuple-element.62) | copy-start | bytes 772
  242.9 6.6 %copy-start.18 = (pred[256]{0:T(512)(128)(4,1)S(1)}, pred[256]{0:T(512)(128)(4,1)}, u32[]{:S(2)}) copy-start(pred[256]{0:T(512)(128)(4,1)} %get-tuple-element.63) | copy-start | bytes 772
  242.9 6.6 %copy-start.19 = (pred[256]{0:T(512)(128)(4,1)S(1)}, pred[256]{0:T(512)(128)(4,1)}, u32[]{:S(2)}) copy-start(pred[256]{0:T(512)(128)(4,1)} %get-tuple-element.64) | copy-start | bytes 772
  242.9 6.6 %copy-start.20 = (pred[256]{0:T(512)(128)(4,1)S(1)}, pred[256]{0:T(512)(128)(4,1)}, u32[]{:S(2)}) copy-start(pred[256]{0:T(512)(128)(4,1)} %get-tuple-element.65) | copy-start | bytes 772
  242.9 6.6 %copy-start.21 = (pred[256]{0:T(512)(128)(4,1)S(1)}, pred[256]{0:T(512)(128)(4,1)}, u32[]{:S(2)}) copy-start(pred[256]{0:T(512)(128)(4,1)} %get-tuple-element.66) | copy-start | bytes 772
  242.9 6.6 %copy-start.22 = (pred[256]{0:T(512)(128)(4,1)S(1)}, pred[256]{0:T(512)(128)(4,1)}, u32[]{:S(2)}) copy-start(pred[256]{0:T(512)(128)(4,1)} %get-tuple-element.67) | copy-start | bytes 772
  242.9 6.6 %copy-start.23 = (pred[256]{0:T(512)(128)(4,1)S(1)}, pred[256]{0:T(512)(128)(4,1)}, u32[]{:S(2)}) copy-start(pred[256]{0:T(512)(128)(4,1)} %get-tuple-element.68) | copy-start | bytes 772
  242.9 6.6 %copy-start.24 = (pred[256]{0:T(512)(128)(4,1)S(1)}, pred[256]{0:T(512)(128)(4,1)}, u32[]{:S(2)}) copy-start(pred[256]{0:T(512)(128)(4,1)} %get-tuple-element.69) | copy-start | bytes 772
  242.9 6.6 %copy-start.25 = (pred[256]{0:T(512)(128)(4,1)S(1)}, pred[256]{0:T(512)(128)(4,1)}, u32[]{:S(2)}) copy-start(pred[256]{0:T(512)(128)(4,1)} %get-tuple-element.70) | copy-start | bytes 772
  242.9 6.6 %copy-start.26 = (pred[256]{0:T(512)(128)(4,1)S(1)}, pred[256]{0:T(512)(128)(4,1)}, u32[]{:S(2)}) copy-start(pred[256]{0:T(512)(128)(4,1)} %get-tuple-element.71) | copy-start | bytes 772
  243.0 6.6 %copy-start.27 = (pred[256]{0:T(512)(128)(4,1)S(1)}, pred[256]{0:T(512)(128)(4,1)}, u32[]{:S(2)}) copy-start(pred[256]{0:T(512)(128)(4,1)} %get-tuple-element.72) | copy-start | bytes 772
  243.0 6.6 %copy-start.28 = (pred[256]{0:T(512)(128)(4,1)S(1)}, pred[256]{0:T(512)(128)(4,1)}, u32[]{:S(2)}) copy-start(pred[256]{0:T(512)(128)(4,1)} %get-tuple-element.73) | copy-start | bytes 772
  243.0 6.6 %copy-start.29 = (pred[256]{0:T(512)(128)(4,1)S(1)}, pred[256]{0:T(512)(128)(4,1)}, u32[]{:S(2)}) copy-start(pred[256]{0:T(512)(128)(4,1)} %get-tuple-element.74) | copy-start | bytes 772
  243.0 6.6 %copy-start.30 = (pred[256]{0:T(512)(128)(4,1)S(1)}, pred[256]{0:T(512)(128)(4,1)}, u32[]{:S(2)}) copy-start(pred[256]{0:T(512)(128)(4,1)} %get-tuple-element.75) | copy-start | bytes 772
  243.0 6.6 %copy-start.31 = (pred[256]{0:T(512)(128)(4,1)S(1)}, pred[256]{0:T(512)(128)(4,1)}, u32[]{:S(2)}) copy-start(pred[256]{0:T(512)(128)(4,1)} %get-tuple-element.76) | copy-start | bytes 772
  243.0 6.6 %copy-start.32 = (pred[256]{0:T(512)(128)(4,1)S(1)}, pred[256]{0:T(512)(128)(4,1)}, u32[]{:S(2)}) copy-start(pred[256]{0:T(512)(128)(4,1)} %get-tuple-element.77) | copy-start | bytes 772
  243.0 6.6 %copy-start.33 = (pred[256]{0:T(512)(128)(4,1)S(1)}, pred[256]{0:T(512)(128)(4,1)}, u32[]{:S(2)}) copy-start(pred[256]{0:T(512)(128)(4,1)} %get-tuple-element.78) | copy-start | bytes 772
  243.0 6.6 %copy-start.34 = (pred[256]{0:T(512)(128)(4,1)S(1)}, pred[256]{0:T(512)(128)(4,1)}, u32[]{:S(2)}) copy-start(pred[256]{0:T(512)(128)(4,1)} %get-tuple-element.79) | copy-start | bytes 772
  243.0 6.6 %copy-start.35 = (pred[256]{0:T(512)(128)(4,1)S(1)}, pred[256]{0:T(512)(128)(4,1)}, u32[]{:S(2)}) copy-start(pred[256]{0:T(512)(128)(4,1)} %get-tuple-element.80) | copy-start | bytes 772
  243.0 6.6 %copy-start.36 = (pred[256]{0:T(512)(128)(4,1)S(1)}, pred[256]{0:T(512)(128)(4,1)}, u32[]{:S(2)}) copy-start(pred[256]{0:T(512)(128)(4,1)} %get-tuple-element.81) | copy-start | bytes 772
  243.1 6.6 %copy-start.37 = (pred[256]{0:T(512)(128)(4,1)S(1)}, pred[256]{0:T(512)(128)(4,1)}, u32[]{:S(2)}) copy-start(pred[256]{0:T(512)(128)(4,1)} %get-tuple-element.38) | copy-start | bytes 772
  243.5 5.8 %collective-permute-start.1 = (bf16[1,15,1536]{2,1,0:T(8,128)(2,1)S(1)}, bf16[1,15,1536]{2,1,0:T(8,128)(2,1)S(1)}, u32[]{:S(2)}, u32[]{:S(2)}) collective-permute-start(bf16[1,15,1536]{2,1,0:T(8,128)(2,1)S(1)} %get-tuple-element.49), channel_id=1, source_target_pairs={{1,0},{2,1},{3,2},{4,3},{5,4},{6,5},{7,6},{8,7},{9,8},{10,9},{11,1... | collective-permute-start | bytes 138248 | tf_op jit(solution)/shard_map/ppermute | solution.py:26
  244.8 4.6 %collective-permute-start = (bf16[1,15,1536]{2,1,0:T(8,128)(2,1)S(1)}, bf16[1,15,1536]{2,1,0:T(8,128)(2,1)S(1)}, u32[]{:S(2)}, u32[]{:S(2)}) collective-permute-start(bf16[1,15,1536]{2,1,0:T(8,128)(2,1)S(1)} %get-tuple-element.48), channel_id=1, source_target_pairs={{0,1},{1,2},{2,3},{3,4},{4,5},{5,6},{6,7},{7,8},{8,9},{9,10},{10,1... | collective-permute-start | bytes 138248 | tf_op jit(solution)/shard_map/ppermute | solution.py:25
  266.6 1.4 copy-start.3
  266.6 1.4 copy-start.42
Sparse Core Ops, SparseCore 0:
  29.1 81.8 all-gather.2
  113.2 123.6 all-gather.4
where the time goes:
time: 283 us; the launch traced here: 280 us
  waiting for transfers between devices  143 us (51%)
  matrix products  50.8 us (18%)
  other arithmetic  42.2 us (15%)
  local copies, waits for them, and re-layouts  25 us (9%)
  between operations  14.1 us (5%)
  starting transfers between devices  4.37 us (2%)
    all_gather x1, waiting for transfers between devices, local(): pieces = lax.all_gather(stacked, 'ctx', axis=1, tiled=True)  77.5 us
    all_gather x1, waiting for transfers between devices, local(): lax.all_gather(conv_in, 'dp', axis=1, tiled=True)  64.9 us
    dot_general x1, matrix products, local(): jnp.einsum('hqk,khd->qhd', exp_scores.astype(jnp.bfloat16), value_piece,...  17.4 us
    reduce_sum x2, other arithmetic, layer_norm(): average = jnp.mean(values, axis=-1, keepdims=True)  17.1 us
    reduce_sum x1, other arithmetic, local(): row_sum = jnp.sum(exp_scores, axis=-1)  16.1 us
    dot_general x1, matrix products, local(): jnp.einsum('qhd,khd->hqk', queries, key_piece, preferred_element_type=jnp...  15.5 us
    unnamed x87, local copies, waits for them, and re-layouts  12.9 us
    slice x1, local copies, waits for them, and re-layouts, local(): key_piece = pieces[0].reshape(length, HEAD_COUNT, HEAD_DIM)  8.4 us
  transfers between devices with their start and end apart: 4, of which 2 were waited for; matrix products, arithmetic and copies ran while one was open for 23% of the time, Pallas kernels for 0%

commit v1 on v0

v1 whole, which is shorter than its diff:
```python
import functools
import math

import jax
import jax.numpy as jnp
import numpy as np
from jax import lax
from jax.experimental import pallas as pl
from jax.experimental.pallas import tpu as pltpu
from jax.sharding import PartitionSpec as P

MODEL_DIM = 1536
HEAD_COUNT = 8
HEAD_DIM = 96
HALF = HEAD_DIM // 2
KERNEL = 31
BLOCK = 128
BLOCKS = 32
LONG = 24
REST = BLOCKS - LONG
HERE = 256
SHARD = 384
EPSILON = 1e-05
MESH = pl.DeviceIdType.MESH
F32 = jnp.float32
BF16 = jnp.bfloat16


def rotation_tables():
    inverse = 10000.0 ** (-np.arange(HALF, dtype=np.float64) / HALF)
    angles = np.arange(LONG * BLOCK, dtype=np.float64)[None, :] * inverse[:, None]
    pair = np.stack([np.cos(angles), np.sin(angles)])
    pair = pair.reshape(2, HALF, LONG, BLOCK).transpose(2, 0, 1, 3)
    return np.ascontiguousarray(pair).astype(np.float32)


def norm(values, gain):
    average = jnp.mean(values, axis=-1, keepdims=True)
    centred = values - average
    variance = jnp.mean(centred * centred, axis=-1, keepdims=True)
    return centred * lax.rsqrt(variance + EPSILON) * gain


def flip(index, off):
    out = index
    for bit in (1, 2, 4):
        if off & bit:
            out = out + bit - 2 * bit * ((index // bit) % 2)
    return out


def kernel(
    x_hbm, ids, attn_gain, wqkv_hbm, wout_hbm, conv_gain, cin_hbm, dw, depth_gain, cout_hbm, tab_hbm,
    out,
    xv, wq, wo, cw, co, tab, normed, send, recv, ks, vs, qs, sbuf, ostage, osend, att, resid, filt, ext, tmp,
    load_sem, wq_sem, a2a_send, a2a_recv, fwd_send, fwd_recv, o_send, o_recv,
    g_send, g_recv, s_send, s_recv, h_send, h_recv,
):
    d = lax.axis_index("dp")
    c = lax.axis_index("ctx")
    chip, core = c // 2, c % 2
    sibling = c + 1 - 2 * core
    z, yh = d // 2, d % 2
    zp, zm, z2 = (z + 1) % 4, (z + 3) % 4, (z + 2) % 4
    other = 1 - yh
    y_lo = chip % 2
    across = (2 * z + other, c + 2 - 4 * y_lo)
    up, down = (2 * zp + yh, c), (2 * zm + yh, c)
    right, left = (d, (c + 1) % 16), (d, (c + 15) % 16)
    peers = [(d, 2 * flip(chip, off) + core) for off in range(8)]

    barrier = pltpu.get_barrier_semaphore()
    cross = (d, lax.select(core == 0, (c + 15) % 16, (c + 1) % 16))
    greeted = peers[1:] + [(d, sibling), across, up, down, cross]
    for device in greeted:
        pl.semaphore_signal(barrier, inc=1, device_id=device, device_id_type=MESH)

    loads = [
        pltpu.make_async_copy(x_hbm.at[0], xv, load_sem.at[0]),
        pltpu.make_async_copy(tab_hbm, tab, load_sem.at[1]),
        pltpu.make_async_copy(wout_hbm, wo, load_sem.at[2]),
        pltpu.make_async_copy(cout_hbm, co, load_sem.at[3]),
        pltpu.make_async_copy(cin_hbm, cw.at[:, pl.ds(SHARD * d, SHARD)], load_sem.at[4]),
    ]
    loads[0].start()
    far = 1 - chip // 4
    groups = (far, chip // 4)
    wq_copies = []
    for stage in range(2):
        for kind in range(3):
            start = pl.multiple_of(768 * kind + SHARD * groups[stage], 128)
            slot = 3 * stage + kind
            copy = pltpu.make_async_copy(
                wqkv_hbm.at[:, pl.ds(start, SHARD)], wq.at[slot], wq_sem.at[slot]
            )
            copy.start()
            wq_copies.append(copy)
        if stage == 0:
            loads[1].start()
    for copy in loads[2:]:
        copy.start()

    def remote(src, dst, device, ssem, rsem):
        return pltpu.make_async_remote_copy(
            src_ref=src, dst_ref=dst, send_sem=ssem, recv_sem=rsem, device_id=device, device_id_type=MESH
        )

    half_rows = pl.ds(pl.multiple_of(768 * core, 768), 768)
    other_rows = pl.ds(pl.multiple_of(768 - 768 * core, 768), 768)

    def part(dd, rows=half_rows):
        return cw.at[rows, pl.ds(pl.multiple_of(SHARD * dd, 128), SHARD)]

    def third(dd, n):
        return part(dd, pl.ds(pl.multiple_of(768 * core + 256 * n, 256), 256))

    def gather_copy(src, dd_dst, device, n):
        return remote(src, dd_dst, device, g_send.at[n], g_recv.at[n])

    own = cin_hbm.at[half_rows]
    a_up, a_down, a_far = 2 * zp + yh, 2 * zm + yh, 2 * z2 + yh
    b_here, b_up, b_down, b_far = 2 * z + other, 2 * zp + other, 2 * zm + other, 2 * z2 + other

    pl.semaphore_wait(barrier, len(greeted))

    step_1 = [
        gather_copy(own, part(d), down, 0),
        gather_copy(own, part(d), across, 1),
        gather_copy(own, part(d), up, 2),
    ]
    for copy in step_1:
        copy.start()

    loads[0].wait()

    def norm_rows(i, _):
        rows = pl.ds(pl.multiple_of(64 * i, 64), 64)
        normed[rows, :] = norm(xv[rows, :].astype(F32), attn_gain[...]).astype(BF16)
        return _

    lax.fori_loop(0, HERE // 64, norm_rows, 0)

    place = []
    for t in range(2):
        mine = ids[0, 2 * c + t]
        earlier = jnp.int32(0)
        for j in range(BLOCKS):
            earlier = earlier + (ids[0, j] < mine).astype(jnp.int32)
        place.append(lax.min(2 * c + t - earlier, LONG - 1))
    loads[1].wait()
    cosine = jnp.concatenate([tab[place[0], 0], tab[place[1], 0]], axis=1)
    sine = jnp.concatenate([tab[place[0], 1], tab[place[1], 1]], axis=1)
    scale = math.log2(math.e) / math.sqrt(HEAD_DIM)

    sends = {}
    for stage in range(2):
        group = groups[stage]
        for kind in range(3):
            slot = 3 * stage + kind
            wq_copies[slot].wait()
            turned = jnp.transpose(jnp.dot(normed[...], wq[slot], preferred_element_type=F32))
            for i in range(4):
                first = turned[96 * i : 96 * i + 48]
                second = turned[96 * i + 48 : 96 * i + 96]
                if kind < 2:
                    first, second = first * cosine - second * sine, second * cosine + first * sine
                if kind == 0:
                    first, second = first * scale, second * scale
                first, second = first.astype(BF16), second.astype(BF16)
                for t in range(2):
                    lanes = slice(BLOCK * t, BLOCK * t + BLOCK)
                    send[4 * group + i, t, kind, 0:48, :] = first[:, lanes]
                    send[4 * group + i, t, kind, 48:96, :] = second[:, lanes]
        for off in (range(4, 8) if stage == 0 else range(1, 4)):
            sends[off] = remote(
                send.at[flip(chip, off)], recv.at[pl.ds(2 * c, 2)], peers[off],
                a2a_send.at[off], a2a_recv.at[off],
            )
            sends[off].start()
    keep = pltpu.make_async_copy(send.at[chip], recv.at[pl.ds(2 * c, 2)], load_sem.at[5])
    keep.start()
    forwards = {
        0: remote(
            send.at[chip, :, pl.ds(1, 2)], recv.at[pl.ds(2 * c, 2), pl.ds(1, 2)], (d, sibling),
            fwd_send.at[0], fwd_recv.at[0],
        )
    }
    forwards[0].start()

    sib_copies = []

    def to_sibling(ref, n):
        copy = remote(ref, ref, (d, sibling), s_send.at[n], s_recv.at[n])
        copy.start()
        sib_copies.append(copy)

    def forward(off):
        source = 2 * flip(chip, off) + core
        remote(
            send.at[0], recv.at[pl.ds(2 * source, 2)], peers[off], a2a_send.at[off], a2a_recv.at[off]
        ).wait_recv()
        block = recv.at[pl.ds(2 * source, 2), pl.ds(1, 2)]
        forwards[off] = remote(block, block, (d, sibling), fwd_send.at[off], fwd_recv.at[off])
        forwards[off].start()

    def gather_wait(ref, n):
        remote(ref, ref, up, g_send.at[n], g_recv.at[n]).wait_recv()

    for off in range(4, 8):
        forward(off)

    gather_wait(part(a_up), 0)
    gather_wait(part(b_here), 1)
    step_2 = [
        gather_copy(part(a_up), part(a_up), down, 3),
        gather_copy(part(a_up), part(a_up), across, 4),
        gather_copy(part(b_here), part(b_here), up, 5),
    ]
    for copy in step_2:
        copy.start()
    gather_wait(part(a_down), 2)
    for off in range(1, 4):
        forward(off)
    to_sibling(part(a_up), 0)
    to_sibling(part(b_here), 1)
    to_sibling(part(a_down), 2)

    keep.wait()
    for off in range(8):
        source = 2 * flip(chip, off) + 1 - core
        block = recv.at[pl.ds(2 * source, 2), pl.ds(1, 2)]
        remote(block, block, (d, sibling), fwd_send.at[off], fwd_recv.at[off]).wait_recv()

    first_long = jnp.int32(0)
    for j in range(REST):
        first_long = first_long + (ids[0, j] != ids[0, BLOCKS // 2]).astype(jnp.int32)
    first_query = jnp.int32(0)
    for u in range(REST // 2):
        first_query = first_query + (4 * (u // 2) + 2 * core + u % 2 < first_long).astype(jnp.int32)

    pad = jnp.zeros((BLOCK - HEAD_DIM, BLOCK), BF16)
    vs[96:112, :] = jnp.ones((16, BLOCKS * BLOCK), BF16)

    def place_keys(j, _):
        block = lax.rem(first_long + j, BLOCKS)
        spot = pl.ds(pl.multiple_of(BLOCK * j, BLOCK), BLOCK)
        ks[spot, :] = jnp.transpose(jnp.concatenate([recv[block, 1], pad], axis=0))
        vs[0:96, spot] = recv[block, 2]
        return _

    lax.fori_loop(0, BLOCKS, place_keys, 0)

    def place_queries(j, _):
        u = lax.rem(first_query + j, 16)
        block = 4 * (u // 2) + 2 * core + u % 2
        qs[:, pl.ds(pl.multiple_of(BLOCK * j, BLOCK), BLOCK)] = jnp.concatenate([recv[block, 0], pad], axis=0)
        return _

    lax.fori_loop(0, 16, place_queries, 0)

    def finish(total, j):
        attended = (total[0:96] / total[96:97]).astype(BF16)
        ostage[2 * j] = attended[:, :BLOCK]
        ostage[2 * j + 1] = attended[:, BLOCK:]

    def long_tile(j, _):
        queries = qs[:, pl.ds(pl.multiple_of(256 * j, 256), 256)]
        top = None
        for k in range(6):
            scores = jnp.dot(ks[512 * k : 512 * k + 512, :], queries, preferred_element_type=F32)
            sbuf[512 * k : 512 * k + 512, :] = scores
            peak = jnp.max(scores, axis=0, keepdims=True)
            top = peak if top is None else jnp.maximum(top, peak)
        total = jnp.zeros((112, 256), F32)
        for k in range(6):
            weights = jnp.exp2(sbuf[512 * k : 512 * k + 512, :] - top).astype(BF16)
            total += jnp.dot(vs[:, 512 * k : 512 * k + 512], weights, preferred_element_type=F32)
        finish(total, j)
        return _

    lax.fori_loop(0, 6, long_tile, 0)

    lane = lax.broadcasted_iota(jnp.int32, (1, 256), 1)
    for j in range(6, 8):
        queries = qs[:, 256 * j : 256 * j + 256]
        marks = []
        for t in range(2):
            u = lax.rem(first_query + 2 * j + t, 16)
            marks.append(ids[0, 4 * (u // 2) + 2 * core + u % 2])
        query_ids = jnp.where(lane < BLOCK, marks[0], marks[1])
        top = None
        for k in range(REST):
            key_id = ids[0, lax.rem(first_long + LONG + k, BLOCKS)]
            rows = pl.ds(BLOCK * (LONG + k), BLOCK)
            scores = jnp.dot(ks[rows, :], queries, preferred_element_type=F32)
            scores = jnp.where(query_ids == key_id, scores, -jnp.inf)
            sbuf[BLOCK * k : BLOCK * k + BLOCK, :] = scores
            peak = jnp.max(scores, axis=0, keepdims=True)
            top = peak if top is None else jnp.maximum(top, peak)
        weights = jnp.exp2(sbuf[0 : REST * BLOCK, :] - top).astype(BF16)
        finish(jnp.dot(vs[:, LONG * BLOCK :], weights, preferred_element_type=F32), j)

    def unplace(u, _):
        osend[u] = ostage[lax.rem(u - first_query + 16, 16)]
        return _

    lax.fori_loop(0, 16, unplace, 0)
    o_copies = {}
    for off in (6, 7, 4, 5, 2, 3, 1):
        to = flip(chip, off)
        o_copies[off] = remote(
            osend.at[pl.ds(2 * to, 2)], att.at[chip], peers[off], o_send.at[off], o_recv.at[off]
        )
        o_copies[off].start()
    o_keep = pltpu.make_async_copy(osend.at[pl.ds(2 * chip, 2)], att.at[chip], load_sem.at[6])
    o_keep.start()

    gather_wait(part(a_far), 3)
    gather_wait(part(b_up), 4)
    gather_wait(part(b_down), 5)
    step_3 = [
        gather_copy(third(a_far, 0), third(a_far, 0), across, 6),
        gather_copy(third(b_up, 1), third(b_up, 1), down, 7),
        gather_copy(third(b_down, 2), third(b_down, 2), up, 8),
    ]
    for copy in step_3:
        copy.start()
    to_sibling(part(a_far), 3)
    to_sibling(part(b_up), 4)
    to_sibling(part(b_down), 5)

    loads[2].wait()
    o_keep.wait()
    for off in range(1, 8):
        source = flip(chip, off)
        remote(att.at[source], att.at[source], peers[off], o_send.at[off], o_recv.at[off]).wait_recv()

    for t in range(2):
        turned = jnp.concatenate([att[h, t] for h in range(8)], axis=0)
        rows = slice(BLOCK * t, BLOCK * t + BLOCK)
        normed[rows, 0:768] = jnp.transpose(turned)

    def add_out(i, _):
        cols = pl.ds(pl.multiple_of(512 * i, 512), 512)
        resid[:, cols] = xv[:, cols].astype(F32) + jnp.dot(
            normed[:, 0:768], wo[:, cols], preferred_element_type=F32
        )
        return _

    lax.fori_loop(0, 3, add_out, 0)

    def norm_residual(i, _):
        rows = pl.ds(pl.multiple_of(64 * i, 64), 64)
        normed[rows, :] = norm(resid[rows, :], conv_gain[...]).astype(BF16)
        return _

    lax.fori_loop(0, HERE // 64, norm_residual, 0)

    for n in range(3):
        gather_wait(third(b_far, n), 6 + n)
    to_sibling(part(b_far), 6)
    loads[4].wait()
    for n, dd in enumerate((a_up, b_here, a_down, a_far, b_up, b_down, b_far)):
        ref = part(dd, other_rows)
        remote(ref, ref, (d, sibling), s_send.at[n], s_recv.at[n]).wait_recv()

    def edge_copies(i):
        cols = pl.ds(pl.multiple_of(256 * i, 256), 256)
        return [
            remote(ext.at[pl.ds(256, 16), cols], ext.at[pl.ds(0, 16), cols], right, h_send.at[0, i], h_recv.at[0, i]),
            remote(ext.at[pl.ds(16, 16), cols], ext.at[pl.ds(272, 16), cols], left, h_send.at[1, i], h_recv.at[1, i]),
        ]

    def gate(i, _):
        cols = pl.ds(pl.multiple_of(256 * i, 256), 256)
        gate_cols = pl.ds(pl.multiple_of(MODEL_DIM + 256 * i, 256), 256)
        value = jnp.dot(normed[...], cw[:, cols], preferred_element_type=F32)
        gates = jnp.dot(normed[...], cw[:, gate_cols], preferred_element_type=F32)
        ext[16:272, cols] = (value * jax.nn.sigmoid(gates)).astype(BF16)
        for copy in edge_copies(i):
            copy.start()
        return _

    lax.fori_loop(0, 6, gate, 0)

    here_0, here_1 = ids[0, 2 * c], ids[0, 2 * c + 1]
    before = ids[0, lax.max(2 * c - 1, 0)]
    after = ids[0, lax.min(2 * c + 2, BLOCKS - 1)]
    inner = here_0 == here_1
    keeps = (
        (jnp.logical_and(c > 0, before == here_0), inner),
        (inner, jnp.logical_and(c < 15, after == here_1)),
    )

    def filter_lanes(i, _):
        cols = pl.ds(pl.multiple_of(BLOCK * i, BLOCK), BLOCK)
        for t in range(2):
            head = ext[BLOCK * t : BLOCK * t + 16, cols].astype(F32)
            tail = ext[BLOCK * t + 144 : BLOCK * t + 160, cols].astype(F32)
            tmp[t, 0:16, :] = jnp.where(keeps[t][0], head, 0.0)
            tmp[t, 16:144, :] = ext[BLOCK * t + 16 : BLOCK * t + 144, cols].astype(F32)
            tmp[t, 144:160, :] = jnp.where(keeps[t][1], tail, 0.0)
            total = jnp.zeros((BLOCK, BLOCK), F32)
            for tap in range(KERNEL):
                total += dw[tap : tap + 1, cols] * tmp[t, tap + 1 : tap + 1 + BLOCK, :]
            filt[BLOCK * t : BLOCK * t + BLOCK, cols] = total
        return _

    def filter_pair(i, _):
        for copy in edge_copies(i):
            copy.wait_recv()
        lax.fori_loop(2 * i, 2 * i + 2, filter_lanes, 0)
        return _

    lax.fori_loop(0, 6, filter_pair, 0)

    def norm_filtered(i, _):
        rows = pl.ds(pl.multiple_of(64 * i, 64), 64)
        values = norm(filt[rows, :], depth_gain[...])
        normed[rows, :] = (values / (1.0 + jnp.exp(-values))).astype(BF16)
        return _

    lax.fori_loop(0, HERE // 64, norm_filtered, 0)

    loads[3].wait()

    def add_conv(i, _):
        cols = pl.ds(pl.multiple_of(512 * i, 512), 512)
        out[0, :, cols] = (
            resid[:, cols] + jnp.dot(normed[...], co[:, cols], preferred_element_type=F32)
        ).astype(BF16)
        return _

    lax.fori_loop(0, 3, add_conv, 0)

    for copy in step_1 + step_2 + step_3 + sib_copies:
        copy.wait_send()
    for copies in (sends, forwards, o_copies):
        for copy in copies.values():
            copy.wait_send()

    def drain(i, _):
        for copy in edge_copies(i):
            copy.wait_send()
        return _

    lax.fori_loop(0, 6, drain, 0)


def local(inputs, block_ids, attn_gain, w_qkv, w_out, conv_gain, conv_in, depthwise_w, depth_gain, conv_out):
    in_hbm = pl.BlockSpec(memory_space=pl.ANY)
    in_vmem = pl.BlockSpec(memory_space=pltpu.VMEM)
    in_smem = pl.BlockSpec(memory_space=pltpu.SMEM)
    dma = pltpu.SemaphoreType.DMA
    return pl.pallas_call(
        kernel,
        out_shape=jax.ShapeDtypeStruct((1, HERE, MODEL_DIM), BF16),
        in_specs=[
            in_hbm, in_smem, in_vmem, in_hbm, in_hbm, in_vmem, in_hbm, in_vmem, in_vmem, in_hbm, in_hbm,
        ],
        out_specs=in_vmem,
        scratch_shapes=[
            pltpu.VMEM((HERE, MODEL_DIM), BF16),
            pltpu.VMEM((6, MODEL_DIM, SHARD), BF16),
            pltpu.VMEM((768, MODEL_DIM), BF16),
            pltpu.VMEM((MODEL_DIM, 2 * MODEL_DIM), BF16),
            pltpu.VMEM((MODEL_DIM, MODEL_DIM), BF16),
            pltpu.VMEM((LONG, 2, HALF, BLOCK), F32),
            pltpu.VMEM((HERE, MODEL_DIM), BF16),
            pltpu.VMEM((8, 2, 3, HEAD_DIM, BLOCK), BF16),
            pltpu.VMEM((BLOCKS, 3, HEAD_DIM, BLOCK), BF16),
            pltpu.VMEM((BLOCKS * BLOCK, BLOCK), BF16),
            pltpu.VMEM((112, BLOCKS * BLOCK), BF16),
            pltpu.VMEM((BLOCK, 16 * BLOCK), BF16),
            pltpu.VMEM((LONG * BLOCK, 256), F32),
            pltpu.VMEM((16, HEAD_DIM, BLOCK), BF16),
            pltpu.VMEM((16, HEAD_DIM, BLOCK), BF16),
            pltpu.VMEM((8, 2, HEAD_DIM, BLOCK), BF16),
            pltpu.VMEM((HERE, MODEL_DIM), F32),
            pltpu.VMEM((HERE, MODEL_DIM), F32),
            pltpu.VMEM((HERE + 32, MODEL_DIM), BF16),
            pltpu.VMEM((2, 160, BLOCK), F32),
            dma((7,)), dma((6,)), dma((8,)), dma((8,)), dma((8,)), dma((8,)), dma((8,)), dma((8,)),
            dma((9,)), dma((9,)), dma((7,)), dma((7,)), dma((2, 6)), dma((2, 6)),
        ],
        compiler_params=pltpu.CompilerParams(
            collective_id=0, has_side_effects=True, vmem_limit_bytes=56 * 1024 * 1024
        ),
        name="conformer",
    )(
        inputs, block_ids, attn_gain[None], w_qkv, w_out, conv_gain[None], conv_in, depthwise_w,
        depth_gain[None], conv_out, jnp.asarray(rotation_tables()),
    )


def solution(mesh):
    return jax.shard_map(
        local,
        mesh=mesh,
        in_specs=(
            P("dp", "ctx", None),
            P("dp", None),
            P(),
            P(),
            P(),
            P(),
            P(None, "dp"),
            P(),
            P(),
            P(),
        ),
        out_specs=P("dp", "ctx", None),
        check_vma=False,
    )
```

time: 283 us -> 70 us (0.25); the launches traced: 280 us -> 69.7 us
  waiting for transfers between devices: 143 us -> 0 us
  Pallas kernels: 0 us -> 63.7 us
  matrix products: 50.8 us -> 0 us
  other arithmetic: 42.2 us -> 0 us
  local copies, waits for them, and re-layouts: 25 us -> 5.94 us
  between operations: 14.1 us -> 0.01 us
  starting transfers between devices: 4.37 us -> 0 us
    all_gather x2 -> x0, waiting for transfers between devices: 142 us -> none  [the longest x1 77.5 us: local(): pieces = lax.all_gather(stacked, 'ctx', axis=1, tiled=True)]
    pallas_call x0 -> x1, Pallas kernels: none -> 63.7 us  [local(): pl.pallas_call(kernel, out_shape=jax.ShapeDtypeStruct((1, HERE, MODEL_DIM...]
    dot_general x6 -> x0, matrix products: 50.8 us -> none  [the longest x1 17.4 us: local(): jnp.einsum('hqk,khd->qhd', exp_scores.astype(jnp.bfloat16), value_piece,...]
    reduce_sum x7 -> x0, other arithmetic: 34.3 us -> none  [the longest x2 17.1 us: layer_norm(): average = jnp.mean(values, axis=-1, keepdims=True)]
    unnamed x87 -> x1, local copies, waits for them, and re-layouts: 12.9 us -> 2.06 us
    slice x5 -> x0, local copies, waits for them, and re-layouts: 10.9 us -> none  [the longest x1 8.4 us: local(): key_piece = pieces[0].reshape(length, HEAD_COUNT, HEAD_DIM)]
    ppermute x2 -> x0, starting transfers between devices: 4.32 us -> none  [the longest x1 3.03 us: extended_2(): before = lax.ppermute(last, axis, up)]
    broadcast_in_dim x0 -> x3, local copies, waits for them, and re-layouts: none -> 3.88 us  [the longest x1 1.3 us: local(): depth_gain[None]]
  transfers between devices with their start and end apart: 4 -> 0, of which waited for: 2 -> 0; matrix products, arithmetic and copies ran while one was open for 23% -> 0% of each run, Pallas kernels for 0% -> 0%
where the time goes in v1:
time: 70 us; the launch traced here: 69.7 us
  Pallas kernels  63.7 us (91%)
  local copies, waits for them, and re-layouts  5.94 us (8%)
    pallas_call x1, Pallas kernels, local(): pl.pallas_call(kernel, out_shape=jax.ShapeDtypeStruct((1, HERE, MODEL_DIM...  63.7 us
    unnamed x1, local copies, waits for them, and re-layouts  2.06 us

profile of v1, /device:TPU:0, one launch (start us, length us, event | category | flops | bytes accessed | tf_op | source)
XLA Modules:
  0.0 69.7 jit_solution(12189625670831335085)
XLA Ops:
  0.0 1.3 %broadcast_in_dim.9.attn_gain = f32[1,1536]{1,0:T(1,128)} reshape(f32[1536]{0:T(1024)} %param.13) | data formatting | bytes 12288 | tf_op jit(solution)/shard_map/broadcast_in_dim | solution.py:491
  1.3 1.3 %broadcast_in_dim.10.conv_gain = f32[1,1536]{1,0:T(1,128)} reshape(f32[1536]{0:T(1024)} %param.16) | data formatting | bytes 12288 | tf_op jit(solution)/shard_map/broadcast_in_dim | solution.py:491
  2.6 1.3 %broadcast_in_dim.11.depth_gain = f32[1,1536]{1,0:T(1,128)} reshape(f32[1536]{0:T(1024)} %param.19) | data formatting | bytes 12288 | tf_op jit(solution)/shard_map/broadcast_in_dim | solution.py:492
  3.9 63.7 %conformer.1 = bf16[1,256,1536]{2,1,0:T(8,128)(2,1)} custom-call(bf16[1,256,1536]{2,1,0:T(8,128)(2,1)} %x_hbm.1, s32[1,32]{1,0:T(1,128)} %ids.1, f32[1,1536]{1,0:T(1,128)} %broadcast_in_dim.9.attn_gain, bf16[1536,2304]{1,0:T(8,128)(2,1)} %wqkv_hbm.1, bf16[768,1536]{1,0:T(8,128)(2,1)} %wout_hbm.1, f32[1,1536]{1,0:T(1,128)} %broadcast_in_dim.10.conv_gain, ...), custom_call_target="tpu_custom_call" | custom-call | tf_op jit(solution)/shard_map/conformer/pallas_call | solution.py:455
  67.6 2.1 %copy.13 = bf16[1,256,1536]{2,1,0:T(8,128)(2,1)} copy(bf16[1,256,1536]{2,1,0:T(8,128)(2,1)} %conformer.1) | data formatting | bytes 1572864
